TPU v7x, 32 devices: a whole 2x2x4 slice. The times are simulated.
32 devices in a mesh: gx: 8 (over z, y), gz: 4 (over x, core).
Axes of the slice: x: 2, y: 2, z: 4, core: 2. Of those that a mesh axis runs over, the one named last changes fastest.
Arguments:
- charge: float32 [32, 1024, 1024], P('gz', 'gx'), may hold values from -24 to 24
- cell_permittivity: float32 [32], replicated, may hold values from 1 to 4
- face_permittivity: float32 [32], replicated, may hold values from 1 to 4
- screening: float32 [32], replicated, may hold values from 0.001 to 0.01
Outputs:
- potential: float32 [32, 1024, 1024], P('gz', 'gx')
All inputs are finite; a program needn't handle non-finite values.
Results may differ from a plain program's by a relative error of at most 0.0003.
Values sent between devices are 32-bit elements; how exact they have to be, the bound alone decides.
A program may use at most 128 MiB of HBM per device.

v0:
```python
import functools

import jax
import jax.numpy as jnp
import ml_dtypes
import numpy as np
from jax import lax
from jax.experimental import pallas as pl
from jax.experimental.pallas import tpu as pltpu
from jax.sharding import PartitionSpec as P

f32 = jnp.float32
bf16 = jnp.bfloat16
LANES = 128
VMEM = 60 * 1024 * 1024
MESH = pl.DeviceIdType.MESH
ROWS = 8
CHUNKS = 4


def frequencies(length):
    col = np.arange(length)
    middle = length // 2
    return np.where(col <= middle, col, col - middle)


def basis_table(length):
    freq = frequencies(length)
    phase = (np.arange(length)[:, None] * freq[None, :]) % length
    angles = phase * (2.0 * np.pi / length)
    cos_part = np.arange(length)[None, :] <= length // 2
    return np.where(cos_part, np.cos(angles), np.sin(angles))


def halves(table):
    high = table.astype(ml_dtypes.bfloat16)
    low = (table - high.astype(np.float64)).astype(ml_dtypes.bfloat16)
    return jnp.asarray(high), jnp.asarray(low)


def mode_weights(length):
    col = np.arange(length)
    edge = (col == 0) | (col == length // 2)
    return np.where(edge, 1.0 / length, 2.0 / length)


def mode_shift(length):
    return (2.0 - 2.0 * np.cos(frequencies(length) * (2.0 * np.pi / length))).astype(np.float32)


def split(value):
    high = value.astype(bf16)
    low = (value - high.astype(f32)).astype(bf16)
    return high, low


def product(left, right):
    dot = functools.partial(jnp.dot, preferred_element_type=f32)
    return dot(left[0], right[0]) + (dot(left[0], right[1]) + dot(left[1], right[0]))


def one_stage(held, pair):
    n = held.shape[0]
    unit, mate, low_cols, low_rows, paired_cols, paired_rows = pair

    def lane_mates(value):
        return jnp.where(low_cols, pltpu.roll(value, LANES - 1, 1), pltpu.roll(value, 1, 1))

    def row_mates(value):
        return jnp.where(low_rows, pltpu.roll(value, n - 1, 0), pltpu.roll(value, 1, 0))

    def rotation(other, axis, low, paired):
        gap = jnp.sum(mate * other - unit * held, axis=axis, keepdims=True)
        twice = jnp.sum(mate * held + unit * other, axis=axis, keepdims=True)
        square = jnp.maximum(gap * gap + twice * twice, 1e-35)
        inverse = lax.rsqrt(square)
        inverse = inverse * (1.5 - 0.5 * square * inverse * inverse)
        inverse = inverse * (1.5 - 0.5 * square * inverse * inverse)
        half = 0.5 + 0.5 * jnp.abs(gap) * inverse
        root = lax.rsqrt(half)
        root = root * (1.5 - 0.5 * half * root * root)
        root = root * (1.5 - 0.5 * half * root * root)
        positive = (gap > 0.0) | ((gap == 0.0) & low)
        sine = 0.5 * jnp.where(positive, twice, -twice) * inverse * root
        return jnp.where(paired, sine, 1.0), jnp.where(paired, half * root, 0.0)

    by_lane = lane_mates(held)
    by_row = row_mates(held)
    by_both = row_mates(by_lane)
    own_row, cross_row = rotation(by_lane, 0, low_cols[:1], paired_cols[:1])
    own_col, cross_col = rotation(by_row, 1, low_rows[:, :1], paired_rows[:, :1])
    return own_col * (own_row * held + cross_row * by_lane) + cross_col * (
        own_row * by_row + cross_row * by_both
    )


def pairings(n):
    shape = (n, LANES)
    row = lax.broadcasted_iota(jnp.int32, shape, 0)
    col = lax.broadcasted_iota(jnp.int32, shape, 1)
    unit = (row == col).astype(f32)

    def pairing(parity):
        def lower(index):
            return ((index + parity) % 2 == 0) & (index < n - 1)

        def upper(index):
            return ((index + parity) % 2 == 1) & (index > 0) & (index < n)

        mate = jnp.where(lower(col), col + 1, jnp.where(upper(col), col - 1, -1))
        return (
            unit,
            (row == mate).astype(f32),
            lower(col),
            lower(row),
            lower(col) | upper(col),
            lower(row) | upper(row),
        )

    return pairing(0), pairing(1)


def one_sweep(held, pairs):
    def two(_, value):
        return one_stage(one_stage(value, pairs[0]), pairs[1])

    return lax.fori_loop(0, held.shape[0] // 2, two, held)


def eigenvectors(cell_col, cell_row, face_col, face_row, low_row, screen_row):
    n = cell_col.shape[0]
    row = lax.broadcasted_iota(jnp.int32, (n, LANES), 0)
    col = lax.broadcasted_iota(jnp.int32, (n, LANES), 1)
    tri = (
        (row == col).astype(f32) * (low_row + face_row + screen_row)
        - (col == row + 1).astype(f32) * face_col
        - (col == row - 1).astype(f32) * face_row
    )
    matrix = tri * (1.0 / jnp.sqrt(cell_col)) * (1.0 / jnp.sqrt(cell_row))
    held = jnp.where(col < n, matrix, (col == row + n).astype(f32))
    pairs = pairings(n)
    held = lax.fori_loop(0, n.bit_length(), lambda _, value: one_sweep(value, pairs), held)
    modes = jnp.where(col < n, pltpu.roll(held, LANES - n, 1), 0.0) / jnp.sqrt(cell_row)
    norm = jnp.sum(cell_row * modes * modes, axis=1, keepdims=True)
    modes = modes * (1.0 / jnp.sqrt(norm))
    slope = pltpu.roll(modes, LANES - 1, 1) - modes
    walls = jnp.where((col == 0) | (col == n - 1), 1.0, 0.0) * face_row[:, n - 1 : n]
    energy = (screen_row + walls) * modes * modes
    energy = energy + jnp.where(col < n - 1, face_row, 0.0) * slope * slope
    return modes, jnp.sum(energy, axis=1, keepdims=True)


def write_tables(modes, fores, backs):
    n = modes.shape[0]
    size = ROWS * n

    def flags(shape, test):
        first = lax.broadcasted_iota(jnp.int32, shape, 0)
        second = lax.broadcasted_iota(jnp.int32, shape, 1)
        return jnp.where(test(first, second), 1.0, 0.0)

    pick_mode = flags((size, n), lambda a, b: a % n == b).astype(bf16)
    spread_mode = flags((n, size), lambda a, b: b % n == a).astype(bf16)
    pick_layer = flags((size, LANES), lambda a, b: a // ROWS == b).astype(bf16)
    spread_layer = flags((LANES, size), lambda a, b: b // ROWS == a).astype(bf16)
    same_fore = flags((size, size), lambda a, b: a // n == b % ROWS)
    same_back = flags((size, size), lambda a, b: a % ROWS == b // n)
    across = (((1,), (1,)), ((), ()))
    for part, fore, back in zip(split(modes), fores, backs):
        turned = jnp.dot(pick_mode, part, preferred_element_type=f32)
        spread = jnp.dot(turned.astype(bf16), spread_layer, preferred_element_type=f32)
        fore[...] = (spread * same_fore).astype(bf16)
        layered = lax.dot_general(pick_layer, part, across, preferred_element_type=f32)
        spread = jnp.dot(layered.astype(bf16), spread_mode, preferred_element_type=f32)
        back[...] = (spread * same_back).astype(bf16)


def raised(base, count):
    value = None
    while count:
        if count & 1:
            value = base if value is None else value * base
        base = base * base
        count >>= 1
    return value


def entering_values(ratio, x_local, blocks, ends):
    across = raised(ratio, x_local)
    around = 1.0 / (1.0 - raised(across, blocks))
    both = ratio * ratio * (1.0 - across * across) / ((1.0 - ratio) * (1.0 + ratio))
    last = ends(blocks - 1, 0)
    for step in reversed(range(blocks - 1)):
        last = ends(step, 0) + across * last
    last = last * around
    tops = []
    enter = last
    for step in reversed(range(blocks)):
        enter = last
        tops.append(ends(step, 1) + both * last)
        last = ends(step, 0) + across * last
    first = tops[-1]
    for top in reversed(tops[:-1]):
        first = top + across * first
    return enter, first * around


def kernel(
    charge, fore_high, fore_low, back_high_in, back_low_in,
    cell_col, cell_row, face_col, face_row, low_row, screen_row, shift_row,
    out,
    sent, got, risen, returned, arrived, result, back_high, back_low,
    to_high, to_low, from_high, from_low, ratio_ref, near, far, turn, ends, linked, flow,
    send_sems, recv_sems, return_sems, arrive_sems, link_send, link_recv, table_sems, out_sems,
):
    depth, x_local, width = charge.shape
    slabs, blocks = sent.shape[1], linked.shape[0]
    layers, part = ratio_ref.shape
    rows = x_local // CHUNKS
    tiles = rows // ROWS
    me, place = lax.axis_index("gz"), lax.axis_index("gx")

    tables = [
        pltpu.make_async_copy(back_high_in, back_high, table_sems.at[0]),
        pltpu.make_async_copy(back_low_in, back_low, table_sems.at[1]),
    ]
    for table in tables:
        table.start()
    barrier = pltpu.get_barrier_semaphore()
    for axis, own, count in (("gz", me, slabs), ("gx", place, blocks)):
        for step in range(1, count):
            other = lax.rem(own + step, count)
            pl.semaphore_signal(barrier, inc=1, device_id={axis: other}, device_id_type=MESH)
    pl.semaphore_wait(barrier, slabs + blocks - 2)

    def send(chunk, step):
        other = lax.rem(me + step, slabs)
        return pltpu.make_async_remote_copy(
            src_ref=sent.at[chunk, step],
            dst_ref=got.at[chunk, step],
            send_sem=send_sems.at[chunk, step],
            recv_sem=recv_sems.at[chunk, step],
            device_id={"gz": other},
            device_id_type=MESH,
        )

    def forward_y(chunk, _):
        start = pl.multiple_of(chunk * rows, rows)
        left = split(charge[:, pl.ds(start, rows), :].reshape(depth * rows, width))
        for step in list(range(1, slabs)) + [0]:
            other = lax.rem(me + step, slabs)
            value = product(left, (fore_high[other], fore_low[other]))
            value = value.reshape(depth, rows, part)
            if step:
                sent[chunk, step] = value
                send(chunk, step).start()
            else:
                got[chunk, 0] = value
        return 0

    lax.fori_loop(0, CHUNKS, forward_y, 0)

    modes, values = eigenvectors(
        cell_col[...], cell_row[...], face_col[...], face_row[...], low_row[...], screen_row[...]
    )
    write_tables(modes, (to_high, to_low), (from_high, from_low))
    total = values + shift_row[...]
    ratio = 2.0 / (2.0 + total + jnp.sqrt(total * (total + 4.0)))
    ratio_ref[...] = ratio

    ends[...] = jnp.zeros_like(ends)
    flow[...] = ratio

    def rise(chunk, _):
        for step in range(1, slabs):
            send(chunk, step).wait_recv()

        def tile(index, _):
            start = pl.multiple_of(index * ROWS, ROWS)
            parts = [
                got[chunk, lax.rem(me + (slabs - slab), slabs), :, pl.ds(start, ROWS), :]
                for slab in range(slabs)
            ]
            block = jnp.concatenate(parts, axis=0).reshape(layers * ROWS, part)
            turn[...] = product((to_high[...], to_low[...]), split(block))
            ratio = ratio_ref[...]
            value, total, power = ends[0], ends[1], flow[...]
            for x in range(ROWS):
                value = turn[x * layers : (x + 1) * layers] + ratio * value
                risen[chunk * rows + start + x] = value
                total = total + power * value
                power = power * ratio
            ends[0] = value
            ends[1] = total
            flow[...] = power
            return 0

        lax.fori_loop(0, tiles, tile, 0)
        return 0

    lax.fori_loop(0, CHUNKS, rise, 0)

    links = []
    for step in range(1, blocks):
        copy = pltpu.make_async_remote_copy(
            src_ref=ends,
            dst_ref=linked.at[step],
            send_sem=link_send.at[step],
            recv_sem=link_recv.at[step],
            device_id={"gx": lax.rem(place + step, blocks)},
            device_id_type=MESH,
        )
        copy.start()
        links.append(copy)
    power = ratio_ref[...]
    for x in range(ROWS):
        near[x] = power
        if x < ROWS - 1:
            power = power * ratio_ref[...]
    for copy in links:
        copy.wait()
    enter, leave = entering_values(
        ratio_ref[...], x_local, blocks,
        lambda step, which: linked[step, which] if step else ends[which],
    )
    flow[...] = leave
    power = near[ROWS - 1]
    for block in range(x_local // ROWS):
        far[block] = enter
        enter = enter * power

    def give_back(chunk, step):
        other = lax.rem(me + step, slabs)
        return pltpu.make_async_remote_copy(
            src_ref=returned.at[chunk, other],
            dst_ref=arrived.at[chunk, step],
            send_sem=return_sems.at[chunk, step],
            recv_sem=arrive_sems.at[chunk, step],
            device_id={"gz": other},
            device_id_type=MESH,
        )

    def fall(turned, _):
        chunk = CHUNKS - 1 - turned

        def tile(turned, _):
            index = tiles - 1 - turned
            start = pl.multiple_of(index * ROWS, ROWS)
            ratio = ratio_ref[...]
            value = flow[...]
            entered = far[chunk * tiles + index]
            for x in reversed(range(ROWS)):
                value = ratio * (risen[chunk * rows + start + x] + near[x] * entered + value)
                turn[x * layers : (x + 1) * layers] = value
            flow[...] = value
            solved = product((from_high[...], from_low[...]), split(turn[...]))
            returned[chunk, :, :, pl.ds(start, ROWS), :] = solved.reshape(
                slabs, depth, ROWS, part
            )
            return 0

        lax.fori_loop(0, tiles, tile, 0)
        for step in range(1, slabs):
            give_back(chunk, step).start()
        return 0

    lax.fori_loop(0, CHUNKS, fall, 0)
    for table in tables:
        table.wait()

    def write(chunk):
        place = pl.ds(pl.multiple_of(chunk * rows, rows), rows)
        return pltpu.make_async_copy(
            result.at[chunk], out.at[:, place, :], out_sems.at[chunk]
        )

    def back_y(turned, _):
        chunk = CHUNKS - 1 - turned
        total = None
        for step in range(slabs):
            if step:
                give_back(chunk, step).wait_recv()
                value = arrived[chunk, step]
            else:
                value = returned[chunk, me]
            source = lax.rem(me + (slabs - step), slabs)
            left = split(value.reshape(depth * rows, part))
            term = product(left, (back_high[source], back_low[source]))
            total = term if total is None else total + term
        result[chunk] = total.reshape(depth, rows, width)
        write(chunk).start()
        return 0

    lax.fori_loop(0, CHUNKS, back_y, 0)

    def settle(chunk, _):
        for step in range(1, slabs):
            send(chunk, step).wait_send()
            give_back(chunk, step).wait_send()
        write(chunk).wait()
        return 0

    lax.fori_loop(0, CHUNKS, settle, 0)


def as_row(value):
    return jnp.pad(value, (0, LANES - value.shape[0]), constant_values=1.0)[None]


def body(charge, cell, face, screening):
    depth, x_local, width = charge.shape
    slabs, blocks = lax.axis_size("gz"), lax.axis_size("gx")
    layers, part, rows = depth * slabs, width // slabs, x_local // CHUNKS
    table = basis_table(width)
    fore = (table * mode_weights(width)[None, :]).reshape(width, slabs, part).transpose(1, 0, 2)
    back = table.T.reshape(slabs, part, width)
    shift_row = lax.dynamic_slice_in_dim(
        jnp.asarray(mode_shift(width)[None]), lax.axis_index("gz") * part, part, 1
    )
    vmem, anywhere = pl.BlockSpec(memory_space=pltpu.VMEM), pl.BlockSpec(memory_space=pl.ANY)
    chunked = pltpu.VMEM((CHUNKS, slabs, depth, rows, part), f32)
    square = pltpu.VMEM((ROWS * layers, ROWS * layers), bf16)
    plane = pltpu.VMEM((layers, part), f32)
    many = pltpu.SemaphoreType.DMA((CHUNKS, slabs))
    return pl.pallas_call(
        kernel,
        out_shape=jax.ShapeDtypeStruct(charge.shape, f32),
        in_specs=[vmem, vmem, vmem, anywhere, anywhere] + [vmem] * 7,
        out_specs=anywhere,
        scratch_shapes=[
            chunked,
            chunked,
            pltpu.VMEM((x_local, layers, part), f32),
            chunked,
            chunked,
            pltpu.VMEM((CHUNKS, depth, rows, width), f32),
            pltpu.VMEM((slabs, part, width), bf16),
            pltpu.VMEM((slabs, part, width), bf16),
            square,
            square,
            square,
            square,
            plane,
            pltpu.VMEM((ROWS, layers, part), f32),
            pltpu.VMEM((x_local // ROWS, layers, part), f32),
            pltpu.VMEM((ROWS * layers, part), f32),
            pltpu.VMEM((2, layers, part), f32),
            pltpu.VMEM((blocks, 2, layers, part), f32),
            plane,
            many,
            many,
            many,
            many,
            pltpu.SemaphoreType.DMA((blocks,)),
            pltpu.SemaphoreType.DMA((blocks,)),
            pltpu.SemaphoreType.DMA((2,)),
            pltpu.SemaphoreType.DMA((CHUNKS,)),
        ],
        compiler_params=pltpu.CompilerParams(
            collective_id=0, has_side_effects=True, vmem_limit_bytes=VMEM
        ),
        cost_estimate=pl.CostEstimate(
            flops=12 * depth * x_local * width * width,
            bytes_accessed=8 * charge.size,
            transcendentals=0,
        ),
        name="precondition",
    )(
        charge, *halves(fore), *halves(back),
        cell[:, None], as_row(cell), face[:, None], as_row(face), as_row(jnp.roll(face, 1)),
        as_row(screening), shift_row,
    )


def solution(mesh):
    in_specs = (P("gz", "gx", None), P(), P(), P())
    out_specs = P("gz", "gx", None)
    return jax.shard_map(body, mesh=mesh, in_specs=in_specs, out_specs=out_specs, check_vma=False)
```

profile of v0, /device:TPU:1, one launch (start us, length us, event | category | flops | bytes accessed | tf_op | source)
XLA Modules:
  0.0 129.6 jit_solution(15009850148791411617)
XLA Ops:
  0.0 1.2 slice.8
  1.2 1.3 constant_dynamic-slice_fusion.shift_row
  2.5 2.0 %pad_bitcast_fusion.2 = (f32[1,128]{1,0:T(1,128)}, f32[1,128]{1,0:T(1,128)}) fusion(f32[32]{0:T(128)} %param.10, f32[31]{0:T(128)} %bitcast.11, f32[1]{0:T(128)} %slice.8), kind=kLoop, calls=%fused_computation.5 | loop fusion | flops 512 | bytes 1280 | tf_op jit(solution)/shard_map/broadcast_in_dim | solution.py:407
  4.5 1.2 pad_bitcast_fusion
  5.7 1.3 %copy.11.face_col = f32[32,1]{1,0:T(8,128)} copy(f32[32,1]{0,1:T(1,128)} %bitcast.12) | data formatting | bytes 256 | tf_op jit(solution)/shard_map/broadcast_in_dim | solution.py:470
  7.0 1.3 %copy.10.cell_col = f32[32,1]{1,0:T(8,128)} copy(f32[32,1]{0,1:T(1,128)} %bitcast.13) | data formatting | bytes 256 | tf_op jit(solution)/shard_map/broadcast_in_dim | solution.py:470
  8.4 116.4 %precondition.1 = f32[8,128,1024]{2,1,0:T(8,128)} custom-call(f32[8,128,1024]{2,1,0:T(8,128)} %charge.1, bf16[4,1024,256]{2,1,0:T(8,128)(2,1)} %constant.23.clone.fore_high, bf16[4,1024,256]{2,1,0:T(8,128)(2,1)} %constant.24.clone.fore_low, bf16[4,256,1024]{2,1,0:T(8,128)(2,1)} %constant.25.clone.back_high_in, ...), custom_call_target="tpu_custom_call" | custom-call | flops 12884901888 | bytes 8388608 | tf_op jit(solution)/shard_map/precondition/pallas_call | solution.py:425
  124.8 4.8 %copy.13 = f32[8,128,1024]{2,1,0:T(8,128)} copy(f32[8,128,1024]{2,1,0:T(8,128)} %precondition.1) | data formatting | bytes 8388608
where the time goes:
time: 132 us; the launch traced here: 130 us
  Pallas kernels  116 us (88%)
  local copies, waits for them, and re-layouts  11.2 us (8%)
  other arithmetic  1.97 us (1%)
    pallas_call x1, Pallas kernels, body(): pl.pallas_call(kernel, out_shape=jax.ShapeDtypeStruct(charge.shape, f32),...  116 us
    unnamed x1, local copies, waits for them, and re-layouts  4.79 us

commit v1 on v0

--- a/solution.py
+++ b/solution.py
@@ -15,6 +15,7 @@
 VMEM = 60 * 1024 * 1024
 MESH = pl.DeviceIdType.MESH
 ROWS = 8
+HALF = 128
 CHUNKS = 4
 
 
@@ -120,14 +121,7 @@
     return pairing(0), pairing(1)
 
 
-def one_sweep(held, pairs):
-    def two(_, value):
-        return one_stage(one_stage(value, pairs[0]), pairs[1])
-
-    return lax.fori_loop(0, held.shape[0] // 2, two, held)
-
-
-def eigenvectors(cell_col, cell_row, face_col, face_row, low_row, screen_row):
+def eigen_start(cell_col, cell_row, face_col, face_row, low_row, screen_row):
     n = cell_col.shape[0]
     row = lax.broadcasted_iota(jnp.int32, (n, LANES), 0)
     col = lax.broadcasted_iota(jnp.int32, (n, LANES), 1)
@@ -137,9 +131,12 @@
         - (col == row - 1).astype(f32) * face_row
     )
     matrix = tri * (1.0 / jnp.sqrt(cell_col)) * (1.0 / jnp.sqrt(cell_row))
-    held = jnp.where(col < n, matrix, (col == row + n).astype(f32))
-    pairs = pairings(n)
-    held = lax.fori_loop(0, n.bit_length(), lambda _, value: one_sweep(value, pairs), held)
+    return jnp.where(col < n, matrix, (col == row + n).astype(f32))
+
+
+def eigen_finish(held, cell_row, face_row, screen_row):
+    n = held.shape[0]
+    col = lax.broadcasted_iota(jnp.int32, (n, LANES), 1)
     modes = jnp.where(col < n, pltpu.roll(held, LANES - n, 1), 0.0) / jnp.sqrt(cell_row)
     norm = jnp.sum(cell_row * modes * modes, axis=1, keepdims=True)
     modes = modes * (1.0 / jnp.sqrt(norm))
@@ -206,16 +203,17 @@
 
 
 def kernel(
-    charge, fore_high, fore_low, back_high_in, back_low_in,
-    cell_col, cell_row, face_col, face_row, low_row, screen_row, shift_row,
+    charge, fore_high, fore_low, back_high_in, back_low_in, cell, face, screening, shift,
     out,
-    sent, got, risen, returned, arrived, result, back_high, back_low,
+    plain, sent, got, risen, returned, arrived, result, back_high, back_low,
     to_high, to_low, from_high, from_low, ratio_ref, near, far, turn, ends, linked, flow,
     send_sems, recv_sems, return_sems, arrive_sems, link_send, link_recv, table_sems, out_sems,
 ):
     depth, x_local, width = charge.shape
-    slabs, blocks = sent.shape[1], linked.shape[0]
-    layers, part = ratio_ref.shape
+    slabs = sent.shape[1]
+    halves_of, layers, half_part = ratio_ref.shape
+    blocks = linked.shape[1]
+    part = halves_of * half_part
     rows = x_local // CHUNKS
     tiles = rows // ROWS
     me, place = lax.axis_index("gz"), lax.axis_index("gx")
@@ -231,140 +229,173 @@
         for step in range(1, count):
             other = lax.rem(own + step, count)
             pl.semaphore_signal(barrier, inc=1, device_id={axis: other}, device_id_type=MESH)
+
+    plain[...] = jnp.ones_like(plain)
+    for index, value in enumerate((cell, face, screening)):
+        plain[index : index + 1, 0:layers] = value[...]
+    cell_row, face_row, screen_row = plain[0:1], plain[1:2], plain[2:3]
+    unit = lax.broadcasted_iota(jnp.int32, (layers, LANES), 0) == lax.broadcasted_iota(
+        jnp.int32, (layers, LANES), 1
+    )
+    cell_col = jnp.sum(jnp.where(unit, cell_row, 0.0), axis=1, keepdims=True)
+    face_col = jnp.sum(jnp.where(unit, face_row, 0.0), axis=1, keepdims=True)
+    lane = lax.broadcasted_iota(jnp.int32, (1, LANES), 1)
+    low_row = jnp.where(lane == 0, face_row[:, layers - 1 : layers], pltpu.roll(face_row, 1, 1))
+    held = eigen_start(cell_col, cell_row, face_col, face_row, low_row, screen_row)
+    pairs = pairings(layers)
+    turns = -(-layers.bit_length() * (layers // 2) // (CHUNKS * slabs))
     pl.semaphore_wait(barrier, slabs + blocks - 2)
 
-    def send(chunk, step):
-        other = lax.rem(me + step, slabs)
+    def send(half, chunk, step):
+        slot = half * CHUNKS + chunk
         return pltpu.make_async_remote_copy(
-            src_ref=sent.at[chunk, step],
-            dst_ref=got.at[chunk, step],
-            send_sem=send_sems.at[chunk, step],
-            recv_sem=recv_sems.at[chunk, step],
-            device_id={"gz": other},
+            src_ref=sent.at[slot, step],
+            dst_ref=got.at[slot, step],
+            send_sem=send_sems.at[slot, step],
+            recv_sem=recv_sems.at[slot, step],
+            device_id={"gz": lax.rem(me + step, slabs)},
             device_id_type=MESH,
         )
 
-    def forward_y(chunk, _):
+    def forward_y(chunk, held):
         start = pl.multiple_of(chunk * rows, rows)
         left = split(charge[:, pl.ds(start, rows), :].reshape(depth * rows, width))
         for step in list(range(1, slabs)) + [0]:
             other = lax.rem(me + step, slabs)
             value = product(left, (fore_high[other], fore_low[other]))
+            for _ in range(turns):
+                held = one_stage(one_stage(held, pairs[0]), pairs[1])
             value = value.reshape(depth, rows, part)
+            for half in range(halves_of):
+                piece = value[:, :, half * half_part : (half + 1) * half_part]
+                if step:
+                    sent[half * CHUNKS + chunk, step] = piece
+                else:
+                    got[half * CHUNKS + chunk, 0] = piece
             if step:
-                sent[chunk, step] = value
-                send(chunk, step).start()
-            else:
-                got[chunk, 0] = value
+                send(0, chunk, step).start()
+        return held
+
+    held = lax.fori_loop(0, CHUNKS, forward_y, held)
+
+    def send_rest(chunk, _):
+        for half in range(1, halves_of):
+            for step in range(1, slabs):
+                send(half, chunk, step).start()
         return 0
 
-    lax.fori_loop(0, CHUNKS, forward_y, 0)
-
-    modes, values = eigenvectors(
-        cell_col[...], cell_row[...], face_col[...], face_row[...], low_row[...], screen_row[...]
-    )
+    lax.fori_loop(0, CHUNKS, send_rest, 0)
+
+    modes, values = eigen_finish(held, cell_row, face_row, screen_row)
     write_tables(modes, (to_high, to_low), (from_high, from_low))
-    total = values + shift_row[...]
+    total = values + shift[me]
     ratio = 2.0 / (2.0 + total + jnp.sqrt(total * (total + 4.0)))
-    ratio_ref[...] = ratio
-
-    ends[...] = jnp.zeros_like(ends)
-    flow[...] = ratio
-
-    def rise(chunk, _):
-        for step in range(1, slabs):
-            send(chunk, step).wait_recv()
-
-        def tile(index, _):
-            start = pl.multiple_of(index * ROWS, ROWS)
-            parts = [
-                got[chunk, lax.rem(me + (slabs - slab), slabs), :, pl.ds(start, ROWS), :]
-                for slab in range(slabs)
-            ]
-            block = jnp.concatenate(parts, axis=0).reshape(layers * ROWS, part)
-            turn[...] = product((to_high[...], to_low[...]), split(block))
-            ratio = ratio_ref[...]
-            value, total, power = ends[0], ends[1], flow[...]
-            for x in range(ROWS):
-                value = turn[x * layers : (x + 1) * layers] + ratio * value
-                risen[chunk * rows + start + x] = value
-                total = total + power * value
-                power = power * ratio
-            ends[0] = value
-            ends[1] = total
-            flow[...] = power
-            return 0
-
-        lax.fori_loop(0, tiles, tile, 0)
-        return 0
-
-    lax.fori_loop(0, CHUNKS, rise, 0)
-
-    links = []
-    for step in range(1, blocks):
-        copy = pltpu.make_async_remote_copy(
-            src_ref=ends,
-            dst_ref=linked.at[step],
-            send_sem=link_send.at[step],
-            recv_sem=link_recv.at[step],
-            device_id={"gx": lax.rem(place + step, blocks)},
-            device_id_type=MESH,
-        )
-        copy.start()
-        links.append(copy)
-    power = ratio_ref[...]
-    for x in range(ROWS):
-        near[x] = power
-        if x < ROWS - 1:
-            power = power * ratio_ref[...]
-    for copy in links:
-        copy.wait()
-    enter, leave = entering_values(
-        ratio_ref[...], x_local, blocks,
-        lambda step, which: linked[step, which] if step else ends[which],
-    )
-    flow[...] = leave
-    power = near[ROWS - 1]
-    for block in range(x_local // ROWS):
-        far[block] = enter
-        enter = enter * power
-
-    def give_back(chunk, step):
+    for half in range(halves_of):
+        ratio_ref[half] = ratio[:, half * half_part : (half + 1) * half_part]
+
+    def give_back(half, chunk, step):
+        slot = half * CHUNKS + chunk
         other = lax.rem(me + step, slabs)
         return pltpu.make_async_remote_copy(
-            src_ref=returned.at[chunk, other],
-            dst_ref=arrived.at[chunk, step],
-            send_sem=return_sems.at[chunk, step],
-            recv_sem=arrive_sems.at[chunk, step],
+            src_ref=returned.at[slot, other],
+            dst_ref=arrived.at[slot, step],
+            send_sem=return_sems.at[slot, step],
+            recv_sem=arrive_sems.at[slot, step],
             device_id={"gz": other},
             device_id_type=MESH,
         )
 
-    def fall(turned, _):
-        chunk = CHUNKS - 1 - turned
-
-        def tile(turned, _):
-            index = tiles - 1 - turned
-            start = pl.multiple_of(index * ROWS, ROWS)
-            ratio = ratio_ref[...]
-            value = flow[...]
-            entered = far[chunk * tiles + index]
-            for x in reversed(range(ROWS)):
-                value = ratio * (risen[chunk * rows + start + x] + near[x] * entered + value)
-                turn[x * layers : (x + 1) * layers] = value
-            flow[...] = value
-            solved = product((from_high[...], from_low[...]), split(turn[...]))
-            returned[chunk, :, :, pl.ds(start, ROWS), :] = solved.reshape(
-                slabs, depth, ROWS, part
+    def solve(half):
+        ends[half] = jnp.zeros(ends.shape[1:], f32)
+        flow[...] = ratio_ref[half]
+
+        def rise(chunk, _):
+            for step in range(1, slabs):
+                send(half, chunk, step).wait_recv()
+
+            def tile(index, _):
+                start = pl.multiple_of(index * ROWS, ROWS)
+                slot = half * CHUNKS + chunk
+                parts = [
+                    got[slot, lax.rem(me + (slabs - slab), slabs), :, pl.ds(start, ROWS), :]
+                    for slab in range(slabs)
+                ]
+                block = jnp.concatenate(parts, axis=0).reshape(layers * ROWS, half_part)
+                turn[...] = product((to_high[...], to_low[...]), split(block))
+                ratio = ratio_ref[half]
+                value, total, power = ends[half, 0], ends[half, 1], flow[...]
+                for x in range(ROWS):
+                    value = turn[x * layers : (x + 1) * layers] + ratio * value
+                    risen[chunk * rows + start + x] = value
+                    total = total + power * value
+                    power = power * ratio
+                ends[half, 0] = value
+                ends[half, 1] = total
+                flow[...] = power
+                return 0
+
+            lax.fori_loop(0, tiles, tile, 0)
+            return 0
+
+        lax.fori_loop(0, CHUNKS, rise, 0)
+
+        links = []
+        for step in range(1, blocks):
+            copy = pltpu.make_async_remote_copy(
+                src_ref=ends.at[half],
+                dst_ref=linked.at[half, step],
+                send_sem=link_send.at[half, step],
+                recv_sem=link_recv.at[half, step],
+                device_id={"gx": lax.rem(place + step, blocks)},
+                device_id_type=MESH,
             )
+            copy.start()
+            links.append(copy)
+        power = ratio_ref[half]
+        for x in range(ROWS):
+            near[x] = power
+            if x < ROWS - 1:
+                power = power * ratio_ref[half]
+        for copy in links:
+            copy.wait()
+        enter, leave = entering_values(
+            ratio_ref[half], x_local, blocks,
+            lambda step, which: linked[half, step, which] if step else ends[half, which],
+        )
+        flow[...] = leave
+        power = near[ROWS - 1]
+        for block in range(x_local // ROWS):
+            far[block] = enter
+            enter = enter * power
+
+        def fall(turned, _):
+            chunk = CHUNKS - 1 - turned
+
+            def tile(turned, _):
+                index = tiles - 1 - turned
+                start = pl.multiple_of(index * ROWS, ROWS)
+                ratio = ratio_ref[half]
+                value = flow[...]
+                entered = far[chunk * tiles + index]
+                for x in reversed(range(ROWS)):
+                    value = ratio * (risen[chunk * rows + start + x] + near[x] * entered + value)
+                    turn[x * layers : (x + 1) * layers] = value
+                flow[...] = value
+                solved = product((from_high[...], from_low[...]), split(turn[...]))
+                returned[half * CHUNKS + chunk, :, :, pl.ds(start, ROWS), :] = solved.reshape(
+                    slabs, depth, ROWS, half_part
+                )
+                return 0
+
+            lax.fori_loop(0, tiles, tile, 0)
+            for step in range(1, slabs):
+                give_back(half, chunk, step).start()
             return 0
 
-        lax.fori_loop(0, tiles, tile, 0)
-        for step in range(1, slabs):
-            give_back(chunk, step).start()
-        return 0
-
-    lax.fori_loop(0, CHUNKS, fall, 0)
+        lax.fori_loop(0, CHUNKS, fall, 0)
+
+    for half in range(halves_of):
+        solve(half)
     for table in tables:
         table.wait()
 
@@ -378,13 +409,17 @@
         chunk = CHUNKS - 1 - turned
         total = None
         for step in range(slabs):
-            if step:
-                give_back(chunk, step).wait_recv()
-                value = arrived[chunk, step]
-            else:
-                value = returned[chunk, me]
+            pieces = []
+            for half in range(halves_of):
+                slot = half * CHUNKS + chunk
+                if step:
+                    give_back(half, chunk, step).wait_recv()
+                    value = arrived[slot, step]
+                else:
+                    value = returned[slot, me]
+                pieces.append(value.reshape(depth * rows, half_part))
             source = lax.rem(me + (slabs - step), slabs)
-            left = split(value.reshape(depth * rows, part))
+            left = split(pieces[0] if halves_of == 1 else jnp.concatenate(pieces, axis=1))
             term = product(left, (back_high[source], back_low[source]))
             total = term if total is None else total + term
         result[chunk] = total.reshape(depth, rows, width)
@@ -394,43 +429,41 @@
     lax.fori_loop(0, CHUNKS, back_y, 0)
 
     def settle(chunk, _):
-        for step in range(1, slabs):
-            send(chunk, step).wait_send()
-            give_back(chunk, step).wait_send()
+        for half in range(halves_of):
+            for step in range(1, slabs):
+                send(half, chunk, step).wait_send()
+                give_back(half, chunk, step).wait_send()
         write(chunk).wait()
         return 0
 
     lax.fori_loop(0, CHUNKS, settle, 0)
-
-
-def as_row(value):
-    return jnp.pad(value, (0, LANES - value.shape[0]), constant_values=1.0)[None]
 
 
 def body(charge, cell, face, screening):
     depth, x_local, width = charge.shape
     slabs, blocks = lax.axis_size("gz"), lax.axis_size("gx")
     layers, part, rows = depth * slabs, width // slabs, x_local // CHUNKS
+    half_part = HALF if part % HALF == 0 else part
+    halves_of = part // half_part
     table = basis_table(width)
     fore = (table * mode_weights(width)[None, :]).reshape(width, slabs, part).transpose(1, 0, 2)
     back = table.T.reshape(slabs, part, width)
-    shift_row = lax.dynamic_slice_in_dim(
-        jnp.asarray(mode_shift(width)[None]), lax.axis_index("gz") * part, part, 1
-    )
+    shift = jnp.asarray(mode_shift(width).reshape(slabs, 1, part))
     vmem, anywhere = pl.BlockSpec(memory_space=pltpu.VMEM), pl.BlockSpec(memory_space=pl.ANY)
-    chunked = pltpu.VMEM((CHUNKS, slabs, depth, rows, part), f32)
+    slots = halves_of * CHUNKS
+    chunked = pltpu.VMEM((slots, slabs, depth, rows, half_part), f32)
     square = pltpu.VMEM((ROWS * layers, ROWS * layers), bf16)
-    plane = pltpu.VMEM((layers, part), f32)
-    many = pltpu.SemaphoreType.DMA((CHUNKS, slabs))
+    many = pltpu.SemaphoreType.DMA((slots, slabs))
     return pl.pallas_call(
         kernel,
         out_shape=jax.ShapeDtypeStruct(charge.shape, f32),
-        in_specs=[vmem, vmem, vmem, anywhere, anywhere] + [vmem] * 7,
+        in_specs=[vmem, vmem, vmem, anywhere, anywhere] + [vmem] * 4,
         out_specs=anywhere,
         scratch_shapes=[
+            pltpu.VMEM((8, LANES), f32),
             chunked,
             chunked,
-            pltpu.VMEM((x_local, layers, part), f32),
+            pltpu.VMEM((x_local, layers, half_part), f32),
             chunked,
             chunked,
             pltpu.VMEM((CHUNKS, depth, rows, width), f32),
@@ -440,19 +473,19 @@
             square,
             square,
             square,
-            plane,
-            pltpu.VMEM((ROWS, layers, part), f32),
-            pltpu.VMEM((x_local // ROWS, layers, part), f32),
-            pltpu.VMEM((ROWS * layers, part), f32),
-            pltpu.VMEM((2, layers, part), f32),
-            pltpu.VMEM((blocks, 2, layers, part), f32),
-            plane,
+            pltpu.VMEM((halves_of, layers, half_part), f32),
+            pltpu.VMEM((ROWS, layers, half_part), f32),
+            pltpu.VMEM((x_local // ROWS, layers, half_part), f32),
+            pltpu.VMEM((ROWS * layers, half_part), f32),
+            pltpu.VMEM((halves_of, 2, layers, half_part), f32),
+            pltpu.VMEM((halves_of, blocks, 2, layers, half_part), f32),
+            pltpu.VMEM((layers, half_part), f32),
             many,
             many,
             many,
             many,
-            pltpu.SemaphoreType.DMA((blocks,)),
-            pltpu.SemaphoreType.DMA((blocks,)),
+            pltpu.SemaphoreType.DMA((halves_of, blocks)),
+            pltpu.SemaphoreType.DMA((halves_of, blocks)),
             pltpu.SemaphoreType.DMA((2,)),
             pltpu.SemaphoreType.DMA((CHUNKS,)),
         ],
@@ -466,9 +499,7 @@
         ),
         name="precondition",
     )(
-        charge, *halves(fore), *halves(back),
-        cell[:, None], as_row(cell), face[:, None], as_row(face), as_row(jnp.roll(face, 1)),
-        as_row(screening), shift_row,
+        charge, *halves(fore), *halves(back), cell[None], face[None], screening[None], shift
     )
 
 

time: 132 us -> 115 us (0.87); the launches traced: 130 us -> 115 us
  local copies, waits for them, and re-layouts: 11.2 us -> 4.79 us
  Pallas kernels: 116 us -> 110 us
  other arithmetic: 1.97 us -> 0 us
    pallas_call x1, Pallas kernels: 116 us -> 110 us  [body(): pl.pallas_call(kernel, out_shape=jax.ShapeDtypeStruct(charge.shape, f32),...]
    broadcast_in_dim x3 -> x0, local copies, waits for them, and re-layouts: 3.9 us -> none  [the longest x1 1.35 us: body(): face[:, None]]
    broadcast_in_dim x1 -> x0, other arithmetic: 1.97 us -> none  [as_row(): jnp.pad(value, (0, LANES - value.shape[0]), constant_values=1.0)[None]]
where the time goes in v1:
time: 115 us
  Pallas kernels  110 us (96%)
  local copies, waits for them, and re-layouts  4.79 us (4%)
    pallas_call x1, Pallas kernels, body(): pl.pallas_call(kernel, out_shape=jax.ShapeDtypeStruct(charge.shape, f32),...  110 us
    unnamed x1, local copies, waits for them, and re-layouts  4.79 us

profile of v1, /device:TPU:1, one launch (start us, length us, event | category | flops | bytes accessed | tf_op | source)
XLA Modules:
  0.0 115.0 jit_solution(10283737269231793205)
XLA Ops:
  0.0 110.2 %precondition.1 = f32[8,128,1024]{2,1,0:T(8,128)} custom-call(f32[8,128,1024]{2,1,0:T(8,128)} %charge.1, bf16[4,1024,256]{2,1,0:T(8,128)(2,1)} %constant.11.clone.fore_high, bf16[4,1024,256]{2,1,0:T(8,128)(2,1)} %constant.12.clone.fore_low, bf16[4,256,1024]{2,1,0:T(8,128)(2,1)} %constant.13.clone.back_high_in, ...), custom_call_target="tpu_custom_call" | custom-call | flops 12884901888 | bytes 8388608 | tf_op jit(solution)/shard_map/precondition/pallas_call | solution.py:457
  110.2 4.8 %copy.11 = f32[8,128,1024]{2,1,0:T(8,128)} copy(f32[8,128,1024]{2,1,0:T(8,128)} %precondition.1) | data formatting | bytes 8388608

commit v2 on v1

--- a/solution.py
+++ b/solution.py
@@ -76,10 +76,8 @@
         square = jnp.maximum(gap * gap + twice * twice, 1e-35)
         inverse = lax.rsqrt(square)
         inverse = inverse * (1.5 - 0.5 * square * inverse * inverse)
-        inverse = inverse * (1.5 - 0.5 * square * inverse * inverse)
         half = 0.5 + 0.5 * jnp.abs(gap) * inverse
         root = lax.rsqrt(half)
-        root = root * (1.5 - 0.5 * half * root * root)
         root = root * (1.5 - 0.5 * half * root * root)
         positive = (gap > 0.0) | ((gap == 0.0) & low)
         sine = 0.5 * jnp.where(positive, twice, -twice) * inverse * root
@@ -203,9 +201,9 @@
 
 
 def kernel(
-    charge, fore_high, fore_low, back_high_in, back_low_in, cell, face, screening, shift,
+    charge_in, fore_high_in, fore_low_in, back_high_in, back_low_in, cell, face, screening, shift,
     out,
-    plain, sent, got, risen, returned, arrived, result, back_high, back_low,
+    charge, fore_high, fore_low, plain, sent, got, risen, returned, arrived, result, back_high, back_low,
     to_high, to_low, from_high, from_low, ratio_ref, near, far, turn, ends, linked, flow,
     send_sems, recv_sems, return_sems, arrive_sems, link_send, link_recv, table_sems, out_sems,
 ):
@@ -222,7 +220,12 @@
         pltpu.make_async_copy(back_high_in, back_high, table_sems.at[0]),
         pltpu.make_async_copy(back_low_in, back_low, table_sems.at[1]),
     ]
-    for table in tables:
+    early = [
+        pltpu.make_async_copy(charge_in, charge, table_sems.at[2]),
+        pltpu.make_async_copy(fore_high_in, fore_high, table_sems.at[3]),
+        pltpu.make_async_copy(fore_low_in, fore_low, table_sems.at[4]),
+    ]
+    for table in early + tables:
         table.start()
     barrier = pltpu.get_barrier_semaphore()
     for axis, own, count in (("gz", me, slabs), ("gx", place, blocks)):
@@ -243,7 +246,14 @@
     low_row = jnp.where(lane == 0, face_row[:, layers - 1 : layers], pltpu.roll(face_row, 1, 1))
     held = eigen_start(cell_col, cell_row, face_col, face_row, low_row, screen_row)
     pairs = pairings(layers)
-    turns = -(-layers.bit_length() * (layers // 2) // (CHUNKS * slabs))
+    turns = -(-(layers.bit_length() - 1) * (layers // 2) // (CHUNKS * slabs))
+
+    def two(_, value):
+        return one_stage(one_stage(value, pairs[0]), pairs[1])
+
+    held = lax.fori_loop(0, layers // 2, two, held)
+    for table in early:
+        table.wait()
     pl.semaphore_wait(barrier, slabs + blocks - 2)
 
     def send(half, chunk, step):
@@ -457,9 +467,12 @@
     return pl.pallas_call(
         kernel,
         out_shape=jax.ShapeDtypeStruct(charge.shape, f32),
-        in_specs=[vmem, vmem, vmem, anywhere, anywhere] + [vmem] * 4,
+        in_specs=[anywhere] * 5 + [vmem] * 4,
         out_specs=anywhere,
         scratch_shapes=[
+            pltpu.VMEM(charge.shape, f32),
+            pltpu.VMEM((slabs, width, part), bf16),
+            pltpu.VMEM((slabs, width, part), bf16),
             pltpu.VMEM((8, LANES), f32),
             chunked,
             chunked,
@@ -486,7 +499,7 @@
             many,
             pltpu.SemaphoreType.DMA((halves_of, blocks)),
             pltpu.SemaphoreType.DMA((halves_of, blocks)),
-            pltpu.SemaphoreType.DMA((2,)),
+            pltpu.SemaphoreType.DMA((5,)),
             pltpu.SemaphoreType.DMA((CHUNKS,)),
         ],
         compiler_params=pltpu.CompilerParams(

time: 115 us -> 108 us (0.939)
  Pallas kernels: 110 us -> 103 us
    pallas_call x1, Pallas kernels: 110 us -> 103 us  [body(): pl.pallas_call(kernel, out_shape=jax.ShapeDtypeStruct(charge.shape, f32),...]
where the time goes in v2:
time: 108 us; the launch traced here: 107 us
  Pallas kernels  103 us (95%)
  local copies, waits for them, and re-layouts  4.79 us (4%)
    pallas_call x1, Pallas kernels, body(): pl.pallas_call(kernel, out_shape=jax.ShapeDtypeStruct(charge.shape, f32),...  103 us
    unnamed x1, local copies, waits for them, and re-layouts  4.79 us

profile of v2, /device:TPU:1, one launch (start us, length us, event | category | flops | bytes accessed | tf_op | source)
XLA Modules:
  0.0 107.5 jit_solution(12948641307130594560)
XLA Ops:
  0.0 102.7 %precondition.1 = f32[8,128,1024]{2,1,0:T(8,128)} custom-call(f32[8,128,1024]{2,1,0:T(8,128)} %charge_in.1, bf16[4,1024,256]{2,1,0:T(8,128)(2,1)} %constant.11.clone.fore_high_in, bf16[4,1024,256]{2,1,0:T(8,128)(2,1)} %constant.12.clone.fore_low_in, bf16[4,256,1024]{2,1,0:T(8,128)(2,1)} %constant.13.clone.back_high_in, ...), custom_call_target="tpu_custom_call" | custom-call | flops 12884901888 | bytes 8388608 | tf_op jit(solution)/shard_map/precondition/pallas_call | solution.py:467
  102.7 4.8 %copy.11 = f32[8,128,1024]{2,1,0:T(8,128)} copy(f32[8,128,1024]{2,1,0:T(8,128)} %precondition.1) | data formatting | bytes 8388608
